TPU v7x, 512 devices: a whole 4x4x16 slice. The times are simulated.
512 devices in a mesh: region: 64 (over z, x), member: 8 (over y, core).
Axes of the slice: x: 4, y: 4, z: 16, core: 2. Of those that a mesh axis runs over, the one named last changes fastest.
Arguments:
- perturbations: bfloat16 [80, 2, 64, 8192], P('member', None, None, 'region'), may hold values from -0.65625 to 0.65625
- control: float32 [80, 64, 8192], P('member', None, 'region'), may hold values from -6 to 6
- vertical_loc: bfloat16 [64, 64], replicated, may hold values from -0.75 to 0.75
- block_kernels: bfloat16 [4, 128, 128], replicated, may hold values from -0.3125 to 0.3125
- loc_pattern: int32 [64, 3], replicated, may hold values from 0 to 3
- obs_region: int32 [65536, 1], P('region'), may hold values from 0 to 63; in each aligned block of 128 rows (0 to 127, 128 to 255, ...) at most 4 rows name the same one
- obs_slot: int32 [65536], P('region'), may hold values from 0 to 1
- obs_cell: int32 [65536], P('region'), may hold values from 0 to 127
- innovations: float32 [64, 65536], P(None, 'region'), may hold values from -12 to 12
- obs_weight: float32 [512, 128, 128], P('region'), may hold values from -0.0375 to 2, as said below
Outputs:
- analysis: float32 [80, 64, 8192], P('member', None, 'region')
Inputs may be any that keep to these rules, and one draw needn't show every extreme that they name: `obs_region`: in each aligned block of 128 rows, no region is named by more than 4 rows. `obs_weight`: each tile is symmetric, and in each row the diagonal entry exceeds the sum of the magnitudes of the other entries.
All inputs are finite; a program needn't handle non-finite values.
Results may differ from a plain program's by a relative error of at most 0.013.
Values may be sent and summed in bfloat16 or wider, within the bound.
A program may use at most 64 MiB of HBM per device.

v0:
```python
import jax
import jax.numpy as jnp
from jax import lax
from jax.sharding import PartitionSpec as P

SLOTS = 2
BLOCK = 128
TILE = 128
ITERS = 2
CELLS_DEV = 128
OBS_DEV = 1024


def padded_2(block, sides, width):
    for axis, dim in sides:
        count = lax.axis_size(axis)
        forward = [(i, i + 1) for i in range(count - 1)]
        backward = [(target, source) for source, target in forward]
        low = lax.ppermute(
            lax.slice_in_dim(block, block.shape[dim] - width, None, axis=dim), axis, forward
        )
        high = lax.ppermute(lax.slice_in_dim(block, 0, width, axis=dim), axis, backward)
        block = jnp.concatenate([low, block, high], axis=dim)
    return block


def pick_kernels(block_kernels, indices):
    kernel_ids = jnp.arange(block_kernels.shape[0], dtype=jnp.int32)
    onehot = (indices[:, None] == kernel_ids[None, :]).astype(jnp.bfloat16)
    return jnp.einsum(
        "bk,kij->bij", onehot, block_kernels, preferred_element_type=jnp.float32
    ).astype(jnp.bfloat16)


def spread_blocks(values, kernel_list, transposed):
    padded = padded_2(values, (("region", 2),), BLOCK)
    member_count, level_count, cell_count = values.shape
    block_count = cell_count // BLOCK
    summed = jnp.zeros((member_count, level_count, block_count, BLOCK), jnp.float32)
    for offset in range(3):
        first_cell = (2 - offset) * BLOCK if transposed else offset * BLOCK
        window = padded[:, :, first_cell : first_cell + cell_count].reshape(
            member_count, level_count, block_count, BLOCK
        )
        if transposed:
            summed = summed + jnp.einsum(
                "mlbj,bkj->mlbk", window, kernel_list[offset], preferred_element_type=jnp.float32
            )
        else:
            summed = summed + jnp.einsum(
                "mlbk,bkj->mlbj", window, kernel_list[offset], preferred_element_type=jnp.float32
            )
    return summed.reshape(member_count, level_count, cell_count)


def route_rows(targets, sub_count, regions, capacity):
    obs_total = targets.shape[0]
    per_sub = obs_total // sub_count
    grouped = targets.reshape(sub_count, per_sub)
    region_ids = jnp.arange(regions, dtype=jnp.int32)
    onehot = (grouped[:, :, None] == region_ids[None, None, :]).astype(jnp.int32)
    before = jnp.cumsum(onehot, axis=1) - onehot
    ranking = jnp.sum(before * onehot, axis=2)
    sub_index = jnp.arange(sub_count, dtype=jnp.int32)[:, None]
    position = (grouped * (sub_count * capacity) + sub_index * capacity + ranking).reshape(
        obs_total
    )
    slot_row = jnp.full((regions * sub_count * capacity,), obs_total, jnp.int32)
    slot_row = slot_row.at[position].set(jnp.arange(obs_total, dtype=jnp.int32))
    return (position, slot_row)


def squared_norm(vector):
    return lax.psum(jnp.sum(vector * vector), ("region", "member"))


def local(
    perturbations,
    control,
    vertical_loc,
    block_kernels,
    loc_pattern,
    obs_region,
    obs_slot,
    obs_cell,
    innovations,
    obs_weight,
):
    regions = lax.axis_size("region")
    members = lax.axis_size("member")
    region_index = lax.axis_index("region")
    member_index = lax.axis_index("member")
    nblocks = CELLS_DEV // BLOCK
    capacity = max(2, 2 * (OBS_DEV // members) // regions)
    group_rows = OBS_DEV // members
    pattern_pad = jnp.pad(loc_pattern, ((1, 1), (0, 0)))
    pattern_rows = lax.dynamic_slice_in_dim(pattern_pad, region_index * nblocks, nblocks + 2, 0)
    forward_list = [
        pick_kernels(block_kernels, pattern_rows[1 : nblocks + 1, offset]) for offset in range(3)
    ]
    backward_list = [
        pick_kernels(block_kernels, pattern_rows[2 - offset : 2 - offset + nblocks, offset])
        for offset in range(3)
    ]
    cell_codes = obs_slot * CELLS_DEV + obs_cell
    targets = obs_region[:, 0]
    sub_count = 1
    first_row = member_index * group_rows
    targets = lax.dynamic_slice_in_dim(targets, first_row, group_rows, 0)
    obs_codes = lax.dynamic_slice_in_dim(cell_codes, first_row, group_rows, 0)
    innovation_rows = lax.dynamic_slice_in_dim(innovations, first_row, group_rows, 1)
    weight_tiles = lax.dynamic_slice_in_dim(
        obs_weight, member_index * (group_rows // TILE), group_rows // TILE, 0
    )
    position, slot_row = route_rows(targets, sub_count, regions, capacity)
    padded_codes = jnp.concatenate([obs_codes, jnp.full((1,), SLOTS * CELLS_DEV, jnp.int32)])
    region_codes = lax.all_to_all(
        padded_codes[slot_row], "region", split_axis=0, concat_axis=0, tiled=True
    )

    def apply_operator(vector, with_innovation):
        spread = spread_blocks(vector.astype(jnp.bfloat16), forward_list, False).astype(
            jnp.bfloat16
        )
        weights = jnp.einsum(
            "lk,mkc->mlc", vertical_loc, spread, preferred_element_type=jnp.float32
        )
        member_sum = jnp.sum(perturbations.astype(jnp.float32) * weights[:, None], axis=0)
        increment = lax.psum(member_sum.astype(jnp.bfloat16), "member").astype(jnp.float32)
        levels_here = increment.shape[1]
        flattened = increment.transpose(1, 0, 2).reshape(levels_here, SLOTS * CELLS_DEV)
        flat_padded = jnp.concatenate([flattened, jnp.zeros((levels_here, 1), jnp.float32)], axis=1)
        sampled = jnp.take(flat_padded, region_codes, axis=1)
        at_holders = lax.all_to_all(
            sampled.astype(jnp.bfloat16), "region", split_axis=1, concat_axis=1, tiled=True
        ).astype(sampled.dtype)
        departures = jnp.take(at_holders, position, axis=1)
        if with_innovation:
            departures = departures - innovation_rows
        obs_count = departures.shape[1]
        weighted = jnp.einsum(
            "ltk,tkj->ltj",
            departures.reshape(levels_here, obs_count // TILE, TILE),
            weight_tiles,
            precision=lax.Precision.HIGHEST,
        ).reshape(levels_here, obs_count)
        weighted_pad = jnp.concatenate([weighted, jnp.zeros((levels_here, 1), jnp.float32)], axis=1)
        returned = jnp.take(weighted_pad, slot_row, axis=1)
        at_regions = lax.all_to_all(
            returned.astype(jnp.bfloat16), "region", split_axis=1, concat_axis=1, tiled=True
        ).astype(returned.dtype)
        adjoint_flat = (
            jnp.zeros((levels_here, SLOTS * CELLS_DEV + 1), jnp.float32)
            .at[:, region_codes]
            .add(at_regions)
        )
        adjoint_part = (
            adjoint_flat[:, : SLOTS * CELLS_DEV]
            .reshape(levels_here, SLOTS, CELLS_DEV)
            .transpose(1, 0, 2)
        )
        adjoint_field = lax.psum(adjoint_part.astype(jnp.bfloat16), "member").astype(jnp.float32)
        projected = jnp.sum(perturbations.astype(jnp.float32) * adjoint_field[None], axis=1).astype(
            jnp.bfloat16
        )
        lifted = jnp.einsum(
            "kl,mkc->mlc", vertical_loc, projected, preferred_element_type=jnp.float32
        ).astype(jnp.bfloat16)
        return vector + spread_blocks(lifted, backward_list, True)

    solution = control
    residual = -apply_operator(control, True)
    direction = residual
    norm_now = squared_norm(residual)
    for iteration in range(ITERS):
        curved = apply_operator(direction, False)
        step_size = norm_now / lax.psum(jnp.sum(direction * curved), ("region", "member"))
        solution = solution + step_size * direction
        if iteration + 1 < ITERS:
            residual = residual - step_size * curved
            norm_next = squared_norm(residual)
            direction = residual + norm_next / norm_now * direction
            norm_now = norm_next
    return solution


def solution(mesh):
    placed = (
        P("member", None, None, "region"),
        P("member", None, "region"),
        P(),
        P(),
        P(),
        P("region", None),
        P("region"),
        P("region"),
        P(None, "region"),
        P("region", None, None),
    )
    return jax.shard_map(
        local, mesh=mesh, in_specs=placed, out_specs=P("member", None, "region"), check_vma=False
    )
```

profile of v0, /device:TPU:1, one launch (start us, length us, event | category | flops | bytes accessed | tf_op | source)
XLA Modules:
  0.0 705.3 jit_solution(5784242501238272621)
XLA Ops:
  0.0 1.1 convert_element_type.222
  1.1 1.3 collective-permute-start.1
  2.4 4.6 collective-permute-start
  8.9 1.0 scatter_custom_fusion
  9.9 1.9 gather_fusion
  12.6 20.4 %all-to-all-start = ((s32[64,4,1]{1,2,0:T(1,128)}), s32[64,4,1]{1,2,0:T(1,128)S(1)}, u32[]{:S(2)}, u32[]{:S(2)}) async-start(s32[64,4,1]{1,2,0:T(1,128)} %bitcast.8), calls=%async_computation | async-start | bytes 65536 | tf_op jit(solution)/shard_map/all_to_all | solution.py:117
  35.0 0.9 fusion.103
  39.4 6.9 all-to-all-done
  48.4 23.6 %psum.70 = bf16[64,256]{0,1:T(8,128)(2,1)S(1)} all-reduce(bf16[64,256]{0,1:T(8,128)(2,1)S(1)} %bitcast.318), channel_id=1, replica_groups=mesh['region'=64,'member'=8] {'member'}, use_global_device_ids=true, to_apply=%region_4.5 | all-reduce | flops 16384 | bytes 65536 | tf_op jit(solution)/shard_map/psum | solution.py:129
  73.7 7.5 %all-to-all-start.1 = ((bf16[64,2,128]{2,1,0:T(2,128)(2,1)}), bf16[64,2,128]{2,1,0:T(2,128)(2,1)S(1)}, u32[]{:S(2)}, u32[]{:S(2)}) async-start(bf16[64,2,128]{2,1,0:T(2,128)(2,1)} %reshape.599), calls=%async_computation.1 | async-start | bytes 65536 | tf_op jit(solution)/shard_map/all_to_all | solution.py:134
  83.6 11.0 %all-to-all-done.1 = bf16[64,2,128]{2,1,0:T(2,128)(2,1)S(1)} async-done(((bf16[64,2,128]{2,1,0:T(2,128)(2,1)}), bf16[64,2,128]{2,1,0:T(2,128)(2,1)S(1)}, u32[]{:S(2)}, u32[]{:S(2)}) %all-to-all-start.1) | async-done | bytes 32800 | tf_op jit(solution)/shard_map/all_to_all | solution.py:134
  95.8 0.9 gather_fusion.3
  97.5 4.6 all-to-all-start.2
  102.1 13.5 %all-to-all-done.2 = bf16[64,2,128]{2,1,0:T(2,128)(2,1)S(1)} async-done(((bf16[64,2,128]{2,1,0:T(2,128)(2,1)}), bf16[64,2,128]{2,1,0:T(2,128)(2,1)S(1)}, u32[]{:S(2)}, u32[]{:S(2)}) %all-to-all-start.2) | async-done | bytes 32800 | tf_op jit(solution)/shard_map/all_to_all | solution.py:149
  115.7 1.5 scatter_custom_fusion.1
  117.3 26.1 %psum.71 = bf16[2,64,128]{2,1,0:T(8,128)(2,1)S(1)} all-reduce(bf16[2,64,128]{2,1,0:T(8,128)(2,1)S(1)} %bitcast.328), channel_id=1, replica_groups=mesh['region'=64,'member'=8] {'member'}, use_global_device_ids=true, to_apply=%region_6.10 | all-reduce | flops 16384 | bytes 65536 | tf_op jit(solution)/shard_map/psum | solution.py:162
  143.8 2.6 collective-permute-start.3
  146.4 1.3 collective-permute-start.2
  148.8 3.6 collective-permute-done.2
  152.7 1.3 collective-permute-start.5
  154.0 4.0 collective-permute-start.4
  158.9 1.3 collective-permute-done.4
  160.8 26.9 %psum.73 = bf16[64,256]{0,1:T(8,128)(2,1)S(1)} all-reduce(bf16[64,256]{0,1:T(8,128)(2,1)S(1)} %bitcast.322), channel_id=1, replica_groups=mesh['region'=64,'member'=8] {'member'}, use_global_device_ids=true, to_apply=%region_11.15 | all-reduce | flops 16384 | bytes 65536 | tf_op jit(solution)/shard_map/psum | solution.py:129
  188.7 27.8 %all_to_all.69 = bf16[64,2,128]{2,1,0:T(2,128)(2,1)S(1)} all-to-all(bf16[64,2,128]{2,1,0:T(2,128)(2,1)S(1)} %reshape.603), channel_id=1, replica_groups=mesh['region'=64,'member'=8] {'region'}, dimensions={0} | all-to-all | bytes 65536 | tf_op jit(solution)/shard_map/all_to_all | solution.py:134
  217.8 0.9 gather_fusion.6
  218.9 17.4 %all_to_all.70 = bf16[64,2,128]{2,1,0:T(2,128)(2,1)S(1)} all-to-all(bf16[64,2,128]{2,1,0:T(2,128)(2,1)S(1)} %reshape.605), channel_id=1, replica_groups=mesh['region'=64,'member'=8] {'region'}, dimensions={0} | all-to-all | bytes 65536 | tf_op jit(solution)/shard_map/all_to_all | solution.py:149
  236.3 1.5 scatter_custom_fusion.2
  238.0 25.9 %psum.74 = bf16[2,64,128]{2,1,0:T(8,128)(2,1)S(1)} all-reduce(bf16[2,64,128]{2,1,0:T(8,128)(2,1)S(1)} %bitcast.329), channel_id=1, replica_groups=mesh['region'=64,'member'=8] {'member'}, use_global_device_ids=true, to_apply=%region_13.17 | all-reduce | flops 16384 | bytes 65536 | tf_op jit(solution)/shard_map/psum | solution.py:162
  264.2 2.6 collective-permute-start.7
  266.8 1.3 collective-permute-start.6
  269.2 3.6 collective-permute-done.6
  272.8 0.9 multiply_reduce_fusion.1
  273.8 105.6 %all-reduce.7 = (f32[]{:T(128)}, f32[]{:T(128)}) all-reduce(f32[]{:T(128)} %get-tuple-element.8, f32[]{:T(128)} %get-tuple-element.6), channel_id=1, replica_groups=mesh['region'=64,'member'=8] {'region','member'}, use_global_device_ids=true, to_apply=%region_9.13 | all-reduce | flops 2 | bytes 16 | tf_op jit(solution)/shard_map/psum | solution.py:74
  381.3 99.4 %psum.76 = f32[]{:T(128)} all-reduce(f32[]{:T(128)} %multiply_reduce_fusion), channel_id=1, replica_groups=mesh['region'=64,'member'=8] {'region','member'}, use_global_device_ids=true, to_apply=%region_18.22 | all-reduce | flops 1 | bytes 8 | tf_op jit(solution)/shard_map/psum | solution.py:74
  482.1 1.3 collective-permute-start.9
  483.4 4.0 collective-permute-start.8
  487.6 1.5 collective-permute-done.9
  490.5 22.6 %psum.77 = bf16[64,256]{0,1:T(8,128)(2,1)S(1)} all-reduce(bf16[64,256]{0,1:T(8,128)(2,1)S(1)} %bitcast.326), channel_id=1, replica_groups=mesh['region'=64,'member'=8] {'member'}, use_global_device_ids=true, to_apply=%region_20.24 | all-reduce | flops 16384 | bytes 65536 | tf_op jit(solution)/shard_map/psum | solution.py:129
  514.2 26.2 %all_to_all.71 = bf16[64,2,128]{2,1,0:T(2,128)(2,1)S(1)} all-to-all(bf16[64,2,128]{2,1,0:T(2,128)(2,1)S(1)} %reshape.607), channel_id=1, replica_groups=mesh['region'=64,'member'=8] {'region'}, dimensions={0} | all-to-all | bytes 65536 | tf_op jit(solution)/shard_map/all_to_all | solution.py:134
  541.7 0.9 gather_fusion.9
  542.8 17.4 %all_to_all.72 = bf16[64,2,128]{2,1,0:T(2,128)(2,1)S(1)} all-to-all(bf16[64,2,128]{2,1,0:T(2,128)(2,1)S(1)} %reshape.609), channel_id=1, replica_groups=mesh['region'=64,'member'=8] {'region'}, dimensions={0} | all-to-all | bytes 65536 | tf_op jit(solution)/shard_map/all_to_all | solution.py:149
  560.2 1.5 scatter_custom_fusion.3
  561.8 25.9 %psum.78 = bf16[2,64,128]{2,1,0:T(8,128)(2,1)S(1)} all-reduce(bf16[2,64,128]{2,1,0:T(8,128)(2,1)S(1)} %bitcast.330), channel_id=1, replica_groups=mesh['region'=64,'member'=8] {'member'}, use_global_device_ids=true, to_apply=%region_22.26 | all-reduce | flops 16384 | bytes 65536 | tf_op jit(solution)/shard_map/psum | solution.py:162
  588.0 2.6 collective-permute-start.11
  590.7 1.3 collective-permute-start.10
  593.1 3.6 collective-permute-done.10
  596.7 0.9 fusion.28
  597.7 105.5 %psum.79 = f32[]{:T(128)} all-reduce(f32[]{:T(128)} %fusion.28), channel_id=1, replica_groups=mesh['region'=64,'member'=8] {'region','member'}, use_global_device_ids=true, to_apply=%region_25.29 | all-reduce | flops 1 | bytes 8 | tf_op jit(solution)/shard_map/psum | solution.py:177
  (134 shorter events, 31.0 us)
Async XLA Ops:
  0.0 95.3 %copy-start = (f32[8,128,128]{2,1,0:T(8,128)S(1)}, f32[8,128,128]{2,1,0:T(8,128)}, u32[]{:S(2)}) copy-start(f32[8,128,128]{2,1,0:T(8,128)} %param.25) | copy-start | bytes 1572868
  1.1 45.4 %collective-permute-start.1 = (bf16[10,64,128]{2,1,0:T(8,128)(2,1)S(1)}, bf16[10,64,128]{2,1,0:T(8,128)(2,1)S(1)}, u32[]{:S(2)}, u32[]{:S(2)}) collective-permute-start(bf16[10,64,128]{2,1,0:T(8,128)(2,1)S(1)} %convert_element_type.222), channel_id=1, source_target_pairs={{8,0},{16,8},{24,16},{32,24},{40,32},{48,40},{56,48},{64,56},{72,6... | collective-permute-start | bytes 491528 | tf_op jit(solution)/shard_map/ppermute | solution.py:22
  2.4 44.3 %collective-permute-start = (bf16[10,64,128]{2,1,0:T(8,128)(2,1)S(1)}, bf16[10,64,128]{2,1,0:T(8,128)(2,1)S(1)}, u32[]{:S(2)}, u32[]{:S(2)}) collective-permute-start(bf16[10,64,128]{2,1,0:T(8,128)(2,1)S(1)} %convert_element_type.222), channel_id=1, source_target_pairs={{0,8},{8,16},{16,24},{24,32},{32,40},{40,48},{48,56},{56,64},{64,7... | collective-permute-start | bytes 491528 | tf_op jit(solution)/shard_map/ppermute | solution.py:19
  7.0 0.7 copy-start.5
  7.0 0.7 copy-start.4
  9.9 25.2 %copy-start.7 = (bf16[4,128,128]{2,1,0:T(8,128)(2,1)S(1)}, bf16[4,128,128]{2,1,0:T(8,128)(2,1)}, u32[]{:S(2)}) copy-start(bf16[4,128,128]{2,1,0:T(8,128)(2,1)} %param.19) | copy-start | bytes 393220
  12.6 33.7 %all-to-all-start = ((s32[64,4,1]{1,2,0:T(1,128)}), s32[64,4,1]{1,2,0:T(1,128)S(1)}, u32[]{:S(2)}, u32[]{:S(2)}) async-start(s32[64,4,1]{1,2,0:T(1,128)} %bitcast.8), calls=%async_computation | async-start | bytes 65536 | tf_op jit(solution)/shard_map/all_to_all | solution.py:117
  33.6 0.7 copy-start.6
  46.5 0.7 copy-start.3
  47.2 1.0 copy-start.1
  73.7 20.9 %all-to-all-start.1 = ((bf16[64,2,128]{2,1,0:T(2,128)(2,1)}), bf16[64,2,128]{2,1,0:T(2,128)(2,1)S(1)}, u32[]{:S(2)}, u32[]{:S(2)}) async-start(bf16[64,2,128]{2,1,0:T(2,128)(2,1)} %reshape.599), calls=%async_computation.1 | async-start | bytes 65536 | tf_op jit(solution)/shard_map/all_to_all | solution.py:134
  97.5 18.1 %all-to-all-start.2 = ((bf16[64,2,128]{2,1,0:T(2,128)(2,1)}), bf16[64,2,128]{2,1,0:T(2,128)(2,1)S(1)}, u32[]{:S(2)}, u32[]{:S(2)}) async-start(bf16[64,2,128]{2,1,0:T(2,128)(2,1)} %reshape.601), calls=%async_computation.2 | async-start | bytes 65536 | tf_op jit(solution)/shard_map/all_to_all | solution.py:149
  143.8 4.8 collective-permute-start.3
  146.4 6.1 collective-permute-start.2
  147.9 4.6 copy-start.2
  152.7 6.1 collective-permute-start.5
  154.0 6.2 collective-permute-start.4
  264.2 4.8 collective-permute-start.7
  266.8 6.1 collective-permute-start.6
  482.1 7.0 collective-permute-start.9
  483.4 6.5 collective-permute-start.8
  588.0 4.8 collective-permute-start.11
  590.7 6.1 collective-permute-start.10
where the time goes:
time: 707 us; the launch traced here: 705 us
  blocking collectives  550 us (78%)
  starting transfers between devices  60.6 us (9%)
  waiting for transfers between devices  48.5 us (7%)
  local copies, waits for them, and re-layouts  19.2 us (3%)
  matrix products  11.3 us (2%)
  other arithmetic  10.8 us (2%)
    psum x2, blocking collectives, squared_norm(): return lax.psum(jnp.sum(vector * vector), ('region', 'member'))  205 us
    psum x1, blocking collectives, local(): lax.psum(jnp.sum(direction * curved), ('region', 'member'))  105 us
    psum x3, blocking collectives, apply_operator(): lax.psum(adjoint_part.astype(jnp.bfloat16), 'member').astype(jnp.float32)  77.9 us
    psum x3, blocking collectives, apply_operator(): lax.psum(member_sum.astype(jnp.bfloat16), 'member').astype(jnp.float32)  73.1 us
    all_to_all x2, blocking collectives, apply_operator(): lax.all_to_all(sampled.astype(jnp.bfloat16), 'region', split_axis=1, conc...  54.1 us
    all_to_all x2, blocking collectives, apply_operator(): lax.all_to_all(returned.astype(jnp.bfloat16), 'region', split_axis=1, con...  34.7 us
    all_to_all x1, starting transfers between devices, local(): lax.all_to_all(padded_codes[slot_row], 'region', split_axis=0, concat_axi...  20.4 us
    ppermute x6, starting transfers between devices, padded_2(): lax.ppermute(lax.slice_in_dim(block, block.shape[dim] - width, None, axis...  20.3 us
  transfers between devices with their start and end apart: 15, of which 13 were waited for; matrix products, arithmetic and copies ran while one was open for 2% of the time, Pallas kernels for 0%

commit v1 on v0

--- a/solution.py
+++ b/solution.py
@@ -2,6 +2,7 @@
 import jax.numpy as jnp
 from jax import lax
 from jax.sharding import PartitionSpec as P
+from jax.lax import all_gather
 
 SLOTS = 2
 BLOCK = 128
@@ -159,7 +160,8 @@
             .reshape(levels_here, SLOTS, CELLS_DEV)
             .transpose(1, 0, 2)
         )
-        adjoint_field = lax.psum(adjoint_part.astype(jnp.bfloat16), "member").astype(jnp.float32)
+        fit_yards = lambda patch: all_gather(patch, "member").sum(axis=0)
+        adjoint_field = fit_yards(adjoint_part.astype(jnp.bfloat16)).astype(jnp.float32)
         projected = jnp.sum(perturbations.astype(jnp.float32) * adjoint_field[None], axis=1).astype(
             jnp.bfloat16
         )

time: 707 us -> 678 us (0.959)
  blocking collectives: 550 us -> 518 us
    psum x3 -> x0, blocking collectives: 77.9 us -> none  [apply_operator(): lax.psum(adjoint_part.astype(jnp.bfloat16), 'member').astype(jnp.float32)]
    all_gather x0 -> x3, blocking collectives: none -> 55.7 us  [apply_operator(): fit_yards = lambda patch: all_gather(patch, 'member').sum(axis=0)]
where the time goes in v1:
time: 678 us; the launch traced here: 677 us
  blocking collectives  518 us (76%)
  starting transfers between devices  60.4 us (9%)
  waiting for transfers between devices  52 us (8%)
  local copies, waits for them, and re-layouts  19.2 us (3%)
  matrix products  11.3 us (2%)
  other arithmetic  10.9 us (2%)
    psum x2, blocking collectives, squared_norm(): return lax.psum(jnp.sum(vector * vector), ('region', 'member'))  202 us
    psum x1, blocking collectives, local(): lax.psum(jnp.sum(direction * curved), ('region', 'member'))  102 us
    psum x3, blocking collectives, apply_operator(): lax.psum(member_sum.astype(jnp.bfloat16), 'member').astype(jnp.float32)  69.5 us
    all_gather x3, blocking collectives, apply_operator(): fit_yards = lambda patch: all_gather(patch, 'member').sum(axis=0)  55.7 us
    all_to_all x2, blocking collectives, apply_operator(): lax.all_to_all(sampled.astype(jnp.bfloat16), 'region', split_axis=1, conc...  54.6 us
    all_to_all x2, blocking collectives, apply_operator(): lax.all_to_all(returned.astype(jnp.bfloat16), 'region', split_axis=1, con...  34.7 us
    all_to_all x1, starting transfers between devices, local(): lax.all_to_all(padded_codes[slot_row], 'region', split_axis=0, concat_axi...  20.4 us
    ppermute x6, starting transfers between devices, padded_2(): lax.ppermute(lax.slice_in_dim(block, block.shape[dim] - width, None, axis...  20.2 us
  transfers between devices with their start and end apart: 15, of which 13 were waited for; matrix products, arithmetic and copies ran while one was open for 2% of the time, Pallas kernels for 0%

profile of v1, /device:TPU:1, one launch (start us, length us, event | category | flops | bytes accessed | tf_op | source)
XLA Modules:
  0.0 676.8 jit_solution(7527511993768962413)
XLA Ops:
  0.0 1.1 convert_element_type.240
  1.1 1.3 collective-permute-start.1
  2.4 4.6 collective-permute-start
  8.9 1.0 scatter_custom_fusion
  9.9 1.9 gather_fusion
  12.6 20.4 %all-to-all-start = ((s32[64,4,1]{1,2,0:T(1,128)}), s32[64,4,1]{1,2,0:T(1,128)S(1)}, u32[]{:S(2)}, u32[]{:S(2)}) async-start(s32[64,4,1]{1,2,0:T(1,128)} %bitcast.8), calls=%async_computation | async-start | bytes 65536 | tf_op jit(solution)/shard_map/all_to_all | solution.py:118
  35.0 0.9 fusion.103
  39.4 6.9 %all-to-all-done = s32[64,4,1]{1,2,0:T(1,128)S(1)} async-done(((s32[64,4,1]{1,2,0:T(1,128)}), s32[64,4,1]{1,2,0:T(1,128)S(1)}, u32[]{:S(2)}, u32[]{:S(2)}) %all-to-all-start) | async-done | bytes 1056 | tf_op jit(solution)/shard_map/all_to_all | solution.py:118
  48.4 23.6 %psum.49 = bf16[64,256]{0,1:T(8,128)(2,1)S(1)} all-reduce(bf16[64,256]{0,1:T(8,128)(2,1)S(1)} %bitcast.324), channel_id=1, replica_groups=mesh['region'=64,'member'=8] {'member'}, use_global_device_ids=true, to_apply=%region_4.5 | all-reduce | flops 16384 | bytes 65536 | tf_op jit(solution)/shard_map/psum | solution.py:130
  73.7 7.5 %all-to-all-start.1 = ((bf16[64,2,128]{2,1,0:T(2,128)(2,1)}), bf16[64,2,128]{2,1,0:T(2,128)(2,1)S(1)}, u32[]{:S(2)}, u32[]{:S(2)}) async-start(bf16[64,2,128]{2,1,0:T(2,128)(2,1)} %reshape.608), calls=%async_computation.1 | async-start | bytes 65536 | tf_op jit(solution)/shard_map/all_to_all | solution.py:135
  83.6 11.0 %all-to-all-done.1 = bf16[64,2,128]{2,1,0:T(2,128)(2,1)S(1)} async-done(((bf16[64,2,128]{2,1,0:T(2,128)(2,1)}), bf16[64,2,128]{2,1,0:T(2,128)(2,1)S(1)}, u32[]{:S(2)}, u32[]{:S(2)}) %all-to-all-start.1) | async-done | bytes 32800 | tf_op jit(solution)/shard_map/all_to_all | solution.py:135
  97.5 4.6 all-to-all-start.2
  102.1 13.5 %all-to-all-done.2 = bf16[64,2,128]{2,1,0:T(2,128)(2,1)S(1)} async-done(((bf16[64,2,128]{2,1,0:T(2,128)(2,1)}), bf16[64,2,128]{2,1,0:T(2,128)(2,1)S(1)}, u32[]{:S(2)}, u32[]{:S(2)}) %all-to-all-start.2) | async-done | bytes 32800 | tf_op jit(solution)/shard_map/all_to_all | solution.py:150
  115.7 1.5 scatter_custom_fusion.1
  117.3 18.8 %all-gather = bf16[16,64,128]{2,1,0:T(8,128)(2,1)S(1)} all-gather(bf16[2,64,128]{2,1,0:T(8,128)(2,1)S(1)} %bitcast.334), channel_id=2, replica_groups=mesh['region'=64,'member'=8] {'member'}, dimensions={0}, use_global_device_ids=true | all-gather | bytes 294912 | tf_op jit(solution)/shard_map/all_gather | solution.py:163
  136.5 2.6 collective-permute-start.3
  139.0 1.3 collective-permute-start.2
  140.5 1.9 collective-permute-done.3
  142.6 3.6 collective-permute-done.2
  146.5 1.3 collective-permute-start.5
  147.8 4.0 collective-permute-start.4
  152.7 1.3 collective-permute-done.4
  154.6 23.2 %psum.51 = bf16[64,256]{0,1:T(8,128)(2,1)S(1)} all-reduce(bf16[64,256]{0,1:T(8,128)(2,1)S(1)} %bitcast.328), channel_id=1, replica_groups=mesh['region'=64,'member'=8] {'member'}, use_global_device_ids=true, to_apply=%region_11.15 | all-reduce | flops 16384 | bytes 65536 | tf_op jit(solution)/shard_map/psum | solution.py:130
  178.9 27.8 %all_to_all.69 = bf16[64,2,128]{2,1,0:T(2,128)(2,1)S(1)} all-to-all(bf16[64,2,128]{2,1,0:T(2,128)(2,1)S(1)} %reshape.612), channel_id=1, replica_groups=mesh['region'=64,'member'=8] {'region'}, dimensions={0} | all-to-all | bytes 65536 | tf_op jit(solution)/shard_map/all_to_all | solution.py:135
  209.0 17.4 %all_to_all.70 = bf16[64,2,128]{2,1,0:T(2,128)(2,1)S(1)} all-to-all(bf16[64,2,128]{2,1,0:T(2,128)(2,1)S(1)} %reshape.614), channel_id=1, replica_groups=mesh['region'=64,'member'=8] {'region'}, dimensions={0} | all-to-all | bytes 65536 | tf_op jit(solution)/shard_map/all_to_all | solution.py:150
  226.5 1.5 scatter_custom_fusion.2
  228.1 18.5 %all-gather.1 = bf16[16,64,128]{2,1,0:T(8,128)(2,1)S(1)} all-gather(bf16[2,64,128]{2,1,0:T(8,128)(2,1)S(1)} %bitcast.335), channel_id=3, replica_groups=mesh['region'=64,'member'=8] {'member'}, dimensions={0}, use_global_device_ids=true | all-gather | bytes 294912 | tf_op jit(solution)/shard_map/all_gather | solution.py:163
  246.9 2.5 collective-permute-start.7
  249.4 1.3 collective-permute-start.6
  250.9 1.9 collective-permute-done.7
  253.0 3.6 collective-permute-done.6
  256.6 0.9 multiply_reduce_fusion.1
  257.6 102.0 %all-reduce.7 = (f32[]{:T(128)}, f32[]{:T(128)}) all-reduce(f32[]{:T(128)} %get-tuple-element.8, f32[]{:T(128)} %get-tuple-element.6), channel_id=1, replica_groups=mesh['region'=64,'member'=8] {'region','member'}, use_global_device_ids=true, to_apply=%region_9.13 | all-reduce | flops 2 | bytes 16 | tf_op jit(solution)/shard_map/psum | solution.py:75
  361.6 99.9 %psum.53 = f32[]{:T(128)} all-reduce(f32[]{:T(128)} %multiply_reduce_fusion), channel_id=1, replica_groups=mesh['region'=64,'member'=8] {'region','member'}, use_global_device_ids=true, to_apply=%region_18.22 | all-reduce | flops 1 | bytes 8 | tf_op jit(solution)/shard_map/psum | solution.py:75
  462.8 1.3 collective-permute-start.9
  464.1 4.0 collective-permute-start.8
  468.3 1.5 collective-permute-done.9
  471.2 22.7 %psum.54 = bf16[64,256]{0,1:T(8,128)(2,1)S(1)} all-reduce(bf16[64,256]{0,1:T(8,128)(2,1)S(1)} %bitcast.332), channel_id=1, replica_groups=mesh['region'=64,'member'=8] {'member'}, use_global_device_ids=true, to_apply=%region_20.24 | all-reduce | flops 16384 | bytes 65536 | tf_op jit(solution)/shard_map/psum | solution.py:130
  495.0 26.8 %all_to_all.71 = bf16[64,2,128]{2,1,0:T(2,128)(2,1)S(1)} all-to-all(bf16[64,2,128]{2,1,0:T(2,128)(2,1)S(1)} %reshape.616), channel_id=1, replica_groups=mesh['region'=64,'member'=8] {'region'}, dimensions={0} | all-to-all | bytes 65536 | tf_op jit(solution)/shard_map/all_to_all | solution.py:135
  524.1 17.4 %all_to_all.72 = bf16[64,2,128]{2,1,0:T(2,128)(2,1)S(1)} all-to-all(bf16[64,2,128]{2,1,0:T(2,128)(2,1)S(1)} %reshape.618), channel_id=1, replica_groups=mesh['region'=64,'member'=8] {'region'}, dimensions={0} | all-to-all | bytes 65536 | tf_op jit(solution)/shard_map/all_to_all | solution.py:150
  541.5 1.5 scatter_custom_fusion.3
  543.1 18.5 %all-gather.2 = bf16[16,64,128]{2,1,0:T(8,128)(2,1)S(1)} all-gather(bf16[2,64,128]{2,1,0:T(8,128)(2,1)S(1)} %bitcast.336), channel_id=4, replica_groups=mesh['region'=64,'member'=8] {'member'}, dimensions={0}, use_global_device_ids=true | all-gather | bytes 294912 | tf_op jit(solution)/shard_map/all_gather | solution.py:163
  562.0 2.6 collective-permute-start.11
  564.6 1.3 collective-permute-start.10
  566.1 1.9 collective-permute-done.11
  568.2 3.6 collective-permute-done.10
  571.8 0.9 fusion.28
  572.8 101.8 %psum.55 = f32[]{:T(128)} all-reduce(f32[]{:T(128)} %fusion.28), channel_id=1, replica_groups=mesh['region'=64,'member'=8] {'region','member'}, use_global_device_ids=true, to_apply=%region_25.29 | all-reduce | flops 1 | bytes 8 | tf_op jit(solution)/shard_map/psum | solution.py:179
  (137 shorter events, 31.5 us)
Async XLA Ops:
  0.0 95.3 %copy-start = (f32[8,128,128]{2,1,0:T(8,128)S(1)}, f32[8,128,128]{2,1,0:T(8,128)}, u32[]{:S(2)}) copy-start(f32[8,128,128]{2,1,0:T(8,128)} %param.25) | copy-start | bytes 1572868
  1.1 45.4 %collective-permute-start.1 = (bf16[10,64,128]{2,1,0:T(8,128)(2,1)S(1)}, bf16[10,64,128]{2,1,0:T(8,128)(2,1)S(1)}, u32[]{:S(2)}, u32[]{:S(2)}) collective-permute-start(bf16[10,64,128]{2,1,0:T(8,128)(2,1)S(1)} %convert_element_type.240), channel_id=1, source_target_pairs={{8,0},{16,8},{24,16},{32,24},{40,32},{48,40},{56,48},{64,56},{72,6... | collective-permute-start | bytes 491528 | tf_op jit(solution)/shard_map/ppermute | solution.py:23
  2.4 44.3 %collective-permute-start = (bf16[10,64,128]{2,1,0:T(8,128)(2,1)S(1)}, bf16[10,64,128]{2,1,0:T(8,128)(2,1)S(1)}, u32[]{:S(2)}, u32[]{:S(2)}) collective-permute-start(bf16[10,64,128]{2,1,0:T(8,128)(2,1)S(1)} %convert_element_type.240), channel_id=1, source_target_pairs={{0,8},{8,16},{16,24},{24,32},{32,40},{40,48},{48,56},{56,64},{64,7... | collective-permute-start | bytes 491528 | tf_op jit(solution)/shard_map/ppermute | solution.py:20
  7.0 0.7 copy-start.5
  7.0 0.7 copy-start.4
  9.9 25.2 %copy-start.7 = (bf16[4,128,128]{2,1,0:T(8,128)(2,1)S(1)}, bf16[4,128,128]{2,1,0:T(8,128)(2,1)}, u32[]{:S(2)}) copy-start(bf16[4,128,128]{2,1,0:T(8,128)(2,1)} %param.19) | copy-start | bytes 393220
  12.6 33.7 %all-to-all-start = ((s32[64,4,1]{1,2,0:T(1,128)}), s32[64,4,1]{1,2,0:T(1,128)S(1)}, u32[]{:S(2)}, u32[]{:S(2)}) async-start(s32[64,4,1]{1,2,0:T(1,128)} %bitcast.8), calls=%async_computation | async-start | bytes 65536 | tf_op jit(solution)/shard_map/all_to_all | solution.py:118
  33.6 0.7 copy-start.6
  46.5 0.7 copy-start.3
  47.2 1.0 copy-start.1
  73.7 20.9 %all-to-all-start.1 = ((bf16[64,2,128]{2,1,0:T(2,128)(2,1)}), bf16[64,2,128]{2,1,0:T(2,128)(2,1)S(1)}, u32[]{:S(2)}, u32[]{:S(2)}) async-start(bf16[64,2,128]{2,1,0:T(2,128)(2,1)} %reshape.608), calls=%async_computation.1 | async-start | bytes 65536 | tf_op jit(solution)/shard_map/all_to_all | solution.py:135
  97.5 18.1 %all-to-all-start.2 = ((bf16[64,2,128]{2,1,0:T(2,128)(2,1)}), bf16[64,2,128]{2,1,0:T(2,128)(2,1)S(1)}, u32[]{:S(2)}, u32[]{:S(2)}) async-start(bf16[64,2,128]{2,1,0:T(2,128)(2,1)} %reshape.610), calls=%async_computation.2 | async-start | bytes 65536 | tf_op jit(solution)/shard_map/all_to_all | solution.py:150
  136.5 6.0 collective-permute-start.3
  139.0 7.2 %collective-permute-start.2 = (bf16[10,64,128]{2,1,0:T(8,128)(2,1)S(1)}, bf16[10,64,128]{2,1,0:T(8,128)(2,1)S(1)}, u32[]{:S(2)}, u32[]{:S(2)}) collective-permute-start(bf16[10,64,128]{2,1,0:T(8,128)(2,1)S(1)} %fusion.19), channel_id=1, source_target_pairs={{8,0},{16,8},{24,16},{32,24},{40,32},{48,40},{56,48},{64,56},{72,6... | collective-permute-start | bytes 491528 | tf_op jit(solution)/shard_map/ppermute | solution.py:23
  140.5 5.7 copy-start.2
  146.5 6.1 collective-permute-start.5
  147.8 6.2 collective-permute-start.4
  246.9 5.9 collective-permute-start.7
  249.4 7.2 %collective-permute-start.6 = (bf16[10,64,128]{2,1,0:T(8,128)(2,1)S(1)}, bf16[10,64,128]{2,1,0:T(8,128)(2,1)S(1)}, u32[]{:S(2)}, u32[]{:S(2)}) collective-permute-start(bf16[10,64,128]{2,1,0:T(8,128)(2,1)S(1)} %fusion.20), channel_id=1, source_target_pairs={{8,0},{16,8},{24,16},{32,24},{40,32},{48,40},{56,48},{64,56},{72,6... | collective-permute-start | bytes 491528 | tf_op jit(solution)/shard_map/ppermute | solution.py:23
  462.8 7.0 %collective-permute-start.9 = (bf16[10,64,128]{2,1,0:T(8,128)(2,1)S(1)}, bf16[10,64,128]{2,1,0:T(8,128)(2,1)S(1)}, u32[]{:S(2)}, u32[]{:S(2)}) collective-permute-start(bf16[10,64,128]{2,1,0:T(8,128)(2,1)S(1)} %fusion.140), channel_id=1, source_target_pairs={{8,0},{16,8},{24,16},{32,24},{40,32},{48,40},{56,48},{64,56},{72,6... | collective-permute-start | bytes 491528 | tf_op jit(solution)/shard_map/ppermute | solution.py:23
  464.1 6.5 collective-permute-start.8
  562.0 6.0 collective-permute-start.11
  564.6 7.2 %collective-permute-start.10 = (bf16[10,64,128]{2,1,0:T(8,128)(2,1)S(1)}, bf16[10,64,128]{2,1,0:T(8,128)(2,1)S(1)}, u32[]{:S(2)}, u32[]{:S(2)}) collective-permute-start(bf16[10,64,128]{2,1,0:T(8,128)(2,1)S(1)} %fusion.21), channel_id=1, source_target_pairs={{8,0},{16,8},{24,16},{32,24},{40,32},{48,40},{56,48},{64,56},{72,6... | collective-permute-start | bytes 491528 | tf_op jit(solution)/shard_map/ppermute | solution.py:23
